TPU v7x, 256 devices: a whole 4x4x8 slice. The times are simulated.
256 devices in a mesh: group: 8 (over z), member: 32 (over x, y, core).
Axes of the slice: x: 4, y: 4, z: 8, core: 2. Of those that a mesh axis runs over, the one named last changes fastest.
Arguments:
- source: bfloat16 [262144, 256], P(('group', 'member')), may hold values from -6 to 6
- target: bfloat16 [65536, 256], P(('group', 'member')), may hold values from -6 to 6
- pair_source: int32 [256, 128], P(('group', 'member')), may hold values from 0 to 3, as said below
- pair_target: int32 [256, 128], P(('group', 'member')), may hold values from 0 to 63, as said below
- pair_count: int32 [256], P(('group', 'member')), may hold values from 4 to 128, as said below
Outputs:
- log_source: float32 [262144], P(('group', 'member'))
- log_target: float32 [65536], P(('group', 'member'))
Inputs may be any that keep to these rules, and one draw needn't show every extreme that they name: `pair_source`: each entry is the device's own source tile, 0 to 3; slots 0 to 3 name each of them once, and no (source tile, window tile) pair stands twice on one device. `pair_target`: window index of the pair's target tile; on every device slot 0 names the device's own target tile (index equal to its member index). `pair_count`: at least 4; in every group one device has exactly 128.
All inputs are finite; a program needn't handle non-finite values.
Results may differ from a plain program's by a relative error of at most 0.0031.
Values may be sent and summed in bfloat16 or wider, within the bound.
A program may use at most 128 MiB of HBM per device.

v0:
```python
import math

import jax
import jax.numpy as jnp
from jax import lax
from jax.sharding import PartitionSpec as P

ITERS = 2


regularizer_strength = 0.05


def shifted(x, axis, by):
    length = lax.axis_size(axis)
    return lax.ppermute(x, axis, [(i, (i + by) % length) for i in range(length)])


def in_one_piece(arrays, axis, dim, along):
    widths = [a.shape[along] for a in arrays]
    both = jnp.concatenate(arrays, axis=along)
    result = lax.all_gather(both, axis, axis=dim, tiled=True)
    return tuple(jnp.split(result, [sum(widths[:k]) for k in range(1, len(widths))], axis=along))


def in_blocks(x, dim, length):
    shape = x.shape
    pieces = x.reshape(*shape[:dim], length, shape[dim] // length, *shape[dim + 1 :])
    return jnp.moveaxis(pieces, dim, 0)


def sum_at_owner(x, axis, dim):
    pieces = in_blocks(x, dim, lax.axis_size(axis))
    arrived = lax.all_to_all(pieces, axis, split_axis=0, concat_axis=0, tiled=True)
    return arrived.sum(axis=0)


def sent_together(arrays, axis, dim, along):
    ends, at = ([], 0)
    for a in arrays[:-1]:
        at += a.shape[along]
        ends.append(at)
    both = jnp.concatenate(arrays, axis=along)
    return tuple(jnp.split(sum_at_owner(both, axis, dim), ends, axis=along))


def in_order(pieces, dim):
    shape = list(pieces.shape[1:])
    shape[dim] *= pieces.shape[0]
    return jnp.moveaxis(pieces, 0, dim).reshape(shape)


def sent_to_all(x, axis):
    length = lax.axis_size(axis)
    return lax.all_to_all(jnp.broadcast_to(x[None], (length, *x.shape)), axis, 0, 0, tiled=True)


def gathered_copies(x, axis, dim):
    return in_order(sent_to_all(x, axis), dim)


def normalize(values):
    floats = values.astype(jnp.float32)
    return (floats / jnp.sqrt(jnp.sum(floats * floats, axis=1, keepdims=True) + 1e-06)).astype(
        jnp.bfloat16
    )


def shards(source, target, pair_source, pair_target, pair_count):
    constituent_entries = lax.axis_size("member")
    cells_per_tile = target.shape[0]
    latent_width = target.shape[1]
    tiles_here = source.shape[0] // cells_per_tile
    unit_source = normalize(source).reshape(tiles_here, cells_per_tile, latent_width)
    unit_target = normalize(target)
    next_target = shifted(unit_target, "group", -1)
    own_window, next_window = in_one_piece((unit_target, next_target), "member", 0, 1)
    window = jnp.concatenate([own_window, next_window], 0).reshape(
        2 * constituent_entries, cells_per_tile, latent_width
    )
    slot_count = pair_source.shape[1]
    block_size = math.gcd(slot_count, 16)
    block_count = slot_count // block_size
    source_slots = pair_source[0]
    window_slots = pair_target[0]
    surviving_indicator = (jnp.arange(slot_count, dtype=jnp.int32) < pair_count[0]).astype(
        jnp.float32
    )
    block_ids = jnp.arange(block_count, dtype=jnp.int32)
    source_blocks = source_slots.reshape(block_count, block_size)
    window_blocks = window_slots.reshape(block_count, block_size)
    keep_blocks = surviving_indicator.reshape(block_count, block_size)
    pick_source = (
        source_slots[:, None] == jnp.arange(tiles_here, dtype=jnp.int32)[None, :]
    ).astype(jnp.float32)
    pick_window = (
        window_slots[:, None] == jnp.arange(2 * constituent_entries, dtype=jnp.int32)[None, :]
    ).astype(jnp.float32)

    def kernels(block_items):
        source_ids, frame_labels, retained_portion = block_items
        own_rows = unit_source[source_ids]
        partners = window[frame_labels]
        similarity_logits = jnp.einsum(
            "pid,pjd->pij", own_rows, partners, preferred_element_type=jnp.float32
        )
        return (
            jnp.exp(similarity_logits / regularizer_strength)
            / cells_per_tile
            * retained_portion[:, None, None]
        ).astype(jnp.bfloat16)

    cached = lax.map(kernels, (source_blocks, window_blocks, keep_blocks))

    def kernel_block(block_items):
        block_index, source_ids, frame_labels, retained_portion = block_items
        return lax.dynamic_index_in_dim(cached, block_index, 0, keepdims=False)

    scale_window = jnp.ones((2 * constituent_entries, cells_per_tile), jnp.float32)
    scale_source = jnp.ones((tiles_here, cells_per_tile), jnp.float32)
    scale_target = jnp.ones((cells_per_tile,), jnp.float32)
    block_inputs = (block_ids, source_blocks, window_blocks, keep_blocks)
    for sweep_number in range(ITERS):

        def row_block(block_items, scale_window=scale_window):
            boltzmann_factor_patches = kernel_block(block_items)
            weights = scale_window[block_items[2]]
            return jnp.sum(
                boltzmann_factor_patches.astype(jnp.float32) * weights[:, None, :], axis=2
            )

        row_parts = lax.map(row_block, block_inputs).reshape(slot_count, cells_per_tile)
        row_sums = jnp.einsum("ps,pi->si", pick_source, row_parts, precision=lax.Precision.HIGHEST)
        scale_source = 1.0 / row_sums

        def column_block(block_items, scale_source=scale_source):
            boltzmann_factor_patches = kernel_block(block_items)
            weights = scale_source[block_items[1]]
            return jnp.sum(
                boltzmann_factor_patches.astype(jnp.float32) * weights[:, :, None], axis=1
            )

        column_parts = lax.map(column_block, block_inputs).reshape(slot_count, cells_per_tile)
        column_terms = jnp.einsum(
            "pw,pj->wj", pick_window, column_parts, precision=lax.Precision.HIGHEST
        )
        column_own, column_next = sent_together(
            (column_terms[:constituent_entries], column_terms[constituent_entries:]), "member", 0, 1
        )
        carried = shifted(column_next, "group", 1)
        columns = (column_own + carried)[0]
        scale_target = float(tiles_here) / columns
        if sweep_number + 1 < ITERS:
            range_scale = gathered_copies(scale_target[None], "member", 0)
            next_scale = shifted(range_scale, "group", -1)
            scale_window = jnp.concatenate([range_scale, next_scale], 0)
    return (jnp.log(scale_source).reshape(tiles_here * cells_per_tile), jnp.log(scale_target))


def solution(mesh):
    placed = (
        P(("group", "member"), None),
        P(("group", "member"), None),
        P(("group", "member"), None),
        P(("group", "member"), None),
        P(("group", "member")),
    )
    return jax.shard_map(
        shards,
        mesh=mesh,
        in_specs=placed,
        out_specs=(P(("group", "member")), P(("group", "member"))),
        check_vma=False,
    )
```

profile of v0, /device:TPU:1, one launch (start us, length us, event | category | flops | bytes accessed | tf_op | source)
XLA Modules:
  0.0 406.5 jit_solution(16225275903400975673)
XLA Ops:
  9.3 6.5 %collective-permute-start = (bf16[256,256]{1,0:T(8,128)(2,1)S(1)}, bf16[256,256]{1,0:T(8,128)(2,1)S(1)}, u32[]{:S(2)}, u32[]{:S(2)}) collective-permute-start(bf16[256,256]{1,0:T(8,128)(2,1)S(1)} %fusion.21), channel_id=1, source_target_pairs={{0,224},{32,0},{64,32},{96,64},{128,96},{160,128},{192,160},{224,1... | collective-permute-start | bytes 393224 | tf_op jit(solution)/shard_map/ppermute | solution.py:16
  15.7 2.2 collective-permute-done
  25.0 52.6 %all-gather.2.cloned.1.call-done = bf16[8192,512]{1,0:T(8,128)(2,1)} async-done(((bf16[256,512]{1,0:T(8,128)(2,1)}), bf16[8192,512]{1,0:T(8,128)(2,1)}) %all-gather.2.cloned.1.call-update) | async-done | bytes 8388624 | tf_op jit(solution)/shard_map/all_gather | solution.py:22
  77.6 3.8 fusion.32
  81.4 24.8 %pad_maximum_fusion = bf16[16384,256]{1,0:T(8,128)(2,1)} fusion(bf16[8192,256]{1,0:T(8,128)(2,1)S(1)} %get-tuple-element.230, bf16[8192,256]{1,0:T(8,128)(2,1)S(1)} %get-tuple-element.229), kind=kLoop, calls=%fused_computation.53 | loop fusion | flops 16777216 | bytes 16777216 | tf_op jit(solution)/shard_map/concatenate | solution.py:78
  106.2 79.5 %while.50 = (s32[]{:T(128)}, bf16[8,16,256,256]{3,2,1,0:T(8,128)(2,1)}, s32[8,16]{1,0:T(8,128)S(1)}, bf16[4,256,256]{2,1,0:T(8,128)(2,1)S(1)}, s32[8,16]{1,0:T(8...) while((s32[]{:T(128)}, bf16[8,16,256,256]{3,2,1,0:T(8,128)(2,1)}, ...), condition=%wide.region_3.4_spmd, body=%wide.region_2.3_spmd.sunk | while | flops 540018816 | bytes 14689565 | solution.py:113
  106.9 5.5 %gather_fusion.1 = bf16[16,256,256]{2,1,0:T(8,128)(2,1)} fusion(bf16[64,256,256]{2,1,0:T(8,128)(2,1)} %get-tuple-element.445, s32[1024]{0:T(1024)S(1)} %pad_clamp_fusion.13), kind=kCustom, calls=%fused_computation.1.clone.1 | custom fusion | bytes 4194368 | tf_op jit(solution)/shard_map/while/body/eval_jaxpr/gather | solution.py:103
  112.4 3.8 bitcast_dynamic-update-slice_fusion.10
  116.9 5.5 %gather_fusion.1 = bf16[16,256,256]{2,1,0:T(8,128)(2,1)} fusion(bf16[64,256,256]{2,1,0:T(8,128)(2,1)} %get-tuple-element.445, s32[1024]{0:T(1024)S(1)} %pad_clamp_fusion.13), kind=kCustom, calls=%fused_computation.1.clone.1 | custom fusion | bytes 4194368 | tf_op jit(solution)/shard_map/while/body/eval_jaxpr/gather | solution.py:103
  122.4 3.7 bitcast_dynamic-update-slice_fusion.10
  126.8 5.5 %gather_fusion.1 = bf16[16,256,256]{2,1,0:T(8,128)(2,1)} fusion(bf16[64,256,256]{2,1,0:T(8,128)(2,1)} %get-tuple-element.445, s32[1024]{0:T(1024)S(1)} %pad_clamp_fusion.13), kind=kCustom, calls=%fused_computation.1.clone.1 | custom fusion | bytes 4194368 | tf_op jit(solution)/shard_map/while/body/eval_jaxpr/gather | solution.py:103
  132.3 3.8 bitcast_dynamic-update-slice_fusion.10
  136.7 5.5 %gather_fusion.1 = bf16[16,256,256]{2,1,0:T(8,128)(2,1)} fusion(bf16[64,256,256]{2,1,0:T(8,128)(2,1)} %get-tuple-element.445, s32[1024]{0:T(1024)S(1)} %pad_clamp_fusion.13), kind=kCustom, calls=%fused_computation.1.clone.1 | custom fusion | bytes 4194368 | tf_op jit(solution)/shard_map/while/body/eval_jaxpr/gather | solution.py:103
  142.2 3.8 bitcast_dynamic-update-slice_fusion.10
  146.7 5.5 %gather_fusion.1 = bf16[16,256,256]{2,1,0:T(8,128)(2,1)} fusion(bf16[64,256,256]{2,1,0:T(8,128)(2,1)} %get-tuple-element.445, s32[1024]{0:T(1024)S(1)} %pad_clamp_fusion.13), kind=kCustom, calls=%fused_computation.1.clone.1 | custom fusion | bytes 4194368 | tf_op jit(solution)/shard_map/while/body/eval_jaxpr/gather | solution.py:103
  152.1 3.8 bitcast_dynamic-update-slice_fusion.10
  156.7 5.5 %gather_fusion.1 = bf16[16,256,256]{2,1,0:T(8,128)(2,1)} fusion(bf16[64,256,256]{2,1,0:T(8,128)(2,1)} %get-tuple-element.445, s32[1024]{0:T(1024)S(1)} %pad_clamp_fusion.13), kind=kCustom, calls=%fused_computation.1.clone.1 | custom fusion | bytes 4194368 | tf_op jit(solution)/shard_map/while/body/eval_jaxpr/gather | solution.py:103
  162.1 3.7 bitcast_dynamic-update-slice_fusion.10
  166.6 5.5 %gather_fusion.1 = bf16[16,256,256]{2,1,0:T(8,128)(2,1)} fusion(bf16[64,256,256]{2,1,0:T(8,128)(2,1)} %get-tuple-element.445, s32[1024]{0:T(1024)S(1)} %pad_clamp_fusion.13), kind=kCustom, calls=%fused_computation.1.clone.1 | custom fusion | bytes 4194368 | tf_op jit(solution)/shard_map/while/body/eval_jaxpr/gather | solution.py:103
  172.0 3.8 bitcast_dynamic-update-slice_fusion.10
  176.5 5.5 %gather_fusion.1 = bf16[16,256,256]{2,1,0:T(8,128)(2,1)} fusion(bf16[64,256,256]{2,1,0:T(8,128)(2,1)} %get-tuple-element.445, s32[1024]{0:T(1024)S(1)} %pad_clamp_fusion.13), kind=kCustom, calls=%fused_computation.1.clone.1 | custom fusion | bytes 4194368 | tf_op jit(solution)/shard_map/while/body/eval_jaxpr/gather | solution.py:103
  182.0 3.8 bitcast_dynamic-update-slice_fusion.10
  185.8 41.2 %while.51 = (s32[]{:T(128)}, f32[8,16,256]{2,1,0:T(8,128)S(1)}, s32[8]{0:T(128)S(1)}, bf16[8,16,256,256]{3,2,1,0:T(8,128)(2,1)}, s32[8,16]{1,0:T(8,128)S(1)}, /*index=5*/s32[]{:T(128)}, f32[]{:T(128)}, s32[]{:T(128)}, s32[]{:T(128)}) while((s32[]{:T(128)}, f32[8,16,256]{2,1,0:T(8,128)S(1)}, s32[8]{0:T(128)S(1)}, ...), condition=%wide.region_6.7_spmd, body=%wide.region_4.6_spmd.sunk | while | flops 3142709 | bytes 2265499 | solution.py:132
  188.7 2.2 fusion.58
  193.8 2.2 fusion.58
  199.0 2.2 fusion.58
  204.1 2.2 fusion.58
  209.3 2.2 fusion.58
  214.4 2.2 fusion.58
  219.6 2.2 fusion.58
  224.7 2.2 fusion.58
  227.3 41.0 %while.52 = (s32[]{:T(128)}, f32[8,16,256]{2,1,0:T(8,128)S(1)}, s32[8]{0:T(128)S(1)}, bf16[8,16,256,256]{3,2,1,0:T(8,128)(2,1)}, s32[8,16]{1,0:T(8,128)S(1)}, /*...) while((s32[]{:T(128)}, f32[8,16,256]{2,1,0:T(8,128)S(1)}, s32[8]{0:T(128)S(1)}, ...), condition=%wide.region_9.10_spmd, body=%wide.region_7.9_spmd.sunk | while | flops 3142709 | bytes 2199959 | solution.py:143
  230.4 1.9 fusion.60
  235.6 1.9 fusion.60
  240.7 1.9 fusion.60
  245.8 1.9 fusion.60
  250.9 1.9 fusion.60
  256.1 1.9 fusion.60
  261.2 1.9 fusion.60
  266.3 1.9 fusion.60
  268.7 12.6 %all_to_all.16 = f32[32,1,512]{2,1,0:T(1,128)S(1)} all-to-all(f32[32,1,512]{2,1,0:T(1,128)S(1)} %copy.7), channel_id=1, replica_groups=mesh['group'=8,'member'=32] {'member'}, dimensions={0} | all-to-all | bytes 131072 | tf_op jit(solution)/shard_map/all_to_all | solution.py:34
  283.0 2.7 collective-permute-done.1
  285.7 11.6 %all_to_all.15 = f32[32,1,256]{2,1,0:T(1,128)S(1)} all-to-all(f32[32,1,256]{2,1,0:T(1,128)S(1)} %broadcast_in_dim.44), channel_id=1, replica_groups=mesh['group'=8,'member'=32] {'member'}, dimensions={0} | all-to-all | bytes 65536 | tf_op jit(solution)/shard_map/all_to_all | solution.py:55
  297.4 1.7 collective-permute-start.2
  300.2 41.1 %while.53 = (s32[]{:T(128)}, f32[8,16,256]{2,1,0:T(8,128)S(1)}, s32[8]{0:T(128)S(1)}, bf16[8,16,256,256]{3,2,1,0:T(8,128)(2,1)}, s32[8,16]{1,0:T(8,128)S(1)}, /*...) while((s32[]{:T(128)}, f32[8,16,256]{2,1,0:T(8,128)S(1)}, s32[8]{0:T(128)S(1)}, ...), condition=%wide.region_13.14_spmd, body=%wide.region_11.13_spmd.sunk | while | flops 3142709 | bytes 2199959 | solution.py:132
  303.1 2.2 fusion.62
  308.2 2.2 fusion.62
  313.3 2.2 fusion.62
  318.5 2.2 fusion.62
  323.6 2.2 fusion.62
  328.7 2.2 fusion.62
  333.9 2.2 fusion.62
  339.0 2.2 fusion.62
  341.6 41.0 %while.54 = (s32[]{:T(128)}, f32[8,16,256]{2,1,0:T(8,128)S(1)}, s32[8]{0:T(128)S(1)}, bf16[8,16,256,256]{3,2,1,0:T(8,128)(2,1)}, s32[8,16]{1,0:T(8,128)S(1)}, /*...) while((s32[]{:T(128)}, f32[8,16,256]{2,1,0:T(8,128)S(1)}, s32[8]{0:T(128)S(1)}, ...), condition=%wide.region_16.17_spmd, body=%wide.region_14.16_spmd.sunk | while | flops 3142709 | bytes 2199959 | solution.py:143
  344.7 1.9 fusion.64
  349.8 1.9 fusion.64
  355.0 1.9 fusion.64
  360.1 1.9 fusion.64
  365.2 1.9 fusion.64
  370.3 1.9 fusion.64
  375.5 1.9 fusion.64
  380.6 1.9 fusion.64
  383.0 12.0 %all_to_all.17 = f32[32,1,512]{2,1,0:T(1,128)S(1)} all-to-all(f32[32,1,512]{2,1,0:T(1,128)S(1)} %copy.8), channel_id=1, replica_groups=mesh['group'=8,'member'=32] {'member'}, dimensions={0} | all-to-all | bytes 131072 | tf_op jit(solution)/shard_map/all_to_all | solution.py:34
  395.7 3.3 collective-permute-done.3
  (260 shorter events, 57.6 us)
Async XLA Ops:
  7.2 70.5 %all-gather.2.cloned.1.call-start = ((), (), s32[]{:S(2)}) async-start(), calls=%async_computation.3 | async-start | bytes 8650752 | tf_op jit(solution)/shard_map/all_gather | solution.py:22
  9.3 8.6 %collective-permute-start = (bf16[256,256]{1,0:T(8,128)(2,1)S(1)}, bf16[256,256]{1,0:T(8,128)(2,1)S(1)}, u32[]{:S(2)}, u32[]{:S(2)}) collective-permute-start(bf16[256,256]{1,0:T(8,128)(2,1)S(1)} %fusion.21), channel_id=1, source_target_pairs={{0,224},{32,0},{64,32},{96,64},{128,96},{160,128},{192,160},{224,1... | collective-permute-start | bytes 393224 | tf_op jit(solution)/shard_map/ppermute | solution.py:16
  185.8 41.2 %copy-start = (s32[1,128]{1,0:T(1,128)S(1)}, s32[1,128]{1,0:T(1,128)}, u32[]{:S(2)}) copy-start(s32[1,128]{1,0:T(1,128)} %param.17) | copy-start | bytes 1540
  227.3 41.0 %copy-start.1 = (s32[1,128]{1,0:T(1,128)S(1)}, s32[1,128]{1,0:T(1,128)}, u32[]{:S(2)}) copy-start(s32[1,128]{1,0:T(1,128)} %param.18) | copy-start | bytes 1540
  281.4 4.3 %collective-permute-start.1 = (f32[1,256]{1,0:T(1,128)S(1)}, f32[1,256]{1,0:T(1,128)S(1)}, u32[]{:S(2)}, u32[]{:S(2)}) collective-permute-start(f32[1,256]{1,0:T(1,128)S(1)} %split.27), channel_id=1, source_target_pairs={{0,32},{32,64},{64,96},{96,128},{128,160},{160,192},{192,224},{224... | collective-permute-start | bytes 3080 | tf_op jit(solution)/shard_map/ppermute | solution.py:16
  297.4 2.8 collective-permute-start.2
  395.0 4.0 collective-permute-start.3
Sparse Core Ops, SparseCore 0:
  18.8 58.7 all-gather.1
where the time goes:
time: 409 us; the launch traced here: 406 us
  other arithmetic  101 us (25%)
  local copies, waits for them, and re-layouts  91.8 us (22%)
  waiting for transfers between devices  61.8 us (15%)
  loops' own time  59.9 us (15%)
  blocking collectives  36.3 us (9%)
  matrix products  31.2 us (8%)
  between operations  14.9 us (4%)
  starting transfers between devices  9.9 us (2%)
    all_gather x1, waiting for transfers between devices, in_one_piece(): result = lax.all_gather(both, axis, axis=dim, tiled=True)  52.6 us
    gather x8, local copies, waits for them, and re-layouts, kernels(): partners = window[frame_labels]  43.6 us
    reduce_sum x16, other arithmetic, row_block(): jnp.sum(boltzmann_factor_patches.astype(jnp.float32) * weights[:, None, :...  35.4 us
    another operation x2, loops' own time, shards(): lax.map(column_block, block_inputs).reshape(slot_count, cells_per_tile)  31.9 us
    reduce_sum x16, other arithmetic, column_block(): jnp.sum(boltzmann_factor_patches.astype(jnp.float32) * weights[:, :, None...  31.1 us
    dot_general x8, matrix products, kernels(): jnp.einsum('pid,pjd->pij', own_rows, partners, preferred_element_type=jnp...  30.1 us
    another operation x2, loops' own time, shards(): lax.map(row_block, block_inputs).reshape(slot_count, cells_per_tile)  27.9 us
    concatenate x1, other arithmetic, shards(): jnp.concatenate([own_window, next_window], 0)  24.8 us
  transfers between devices with their start and end apart: 5, of which 5 were waited for; matrix products, arithmetic and copies ran while one was open for 2% of the time, Pallas kernels for 0%

commit v1 on v0

v1 whole, which is shorter than its diff:
```python
import jax
import jax.numpy as jnp
from jax import lax
from jax.experimental import pallas as pl
from jax.experimental.pallas import tpu as pltpu
from jax.sharding import PartitionSpec as P

MESH = pl.DeviceIdType.MESH
F32, BF16 = jnp.float32, jnp.bfloat16
ROWS_BY_ROWS = (((1,), (1,)), ((), ()))
ROWS_BY_COLUMNS = (((1,), (0,)), ((), ()))
SHARPNESS = 20.0 * 1.4426950408889634
TILE = 256
SOURCES = 4
WINDOW = 64
SLOTS = 128
ORDER = ((0, 0), (0, 1), (0, 3), (1, 0), (0, 2), (1, 1), (1, 3), (1, 2))
BLOCK = {ra: i for i, ra in enumerate(ORDER)}


def place(block, kind, b):
    return block * 8 + kind * 4 + b


def unit(values):
    floats = values.astype(F32)
    return (floats * lax.rsqrt(jnp.sum(floats * floats, axis=1, keepdims=True) + 1e-06)).astype(BF16)


def high_low(x):
    high = x.astype(BF16)
    return high, (x - high.astype(F32)).astype(BF16)


def stacked(x):
    high = x.astype(BF16).astype(F32)
    both = [jnp.broadcast_to(high, (8, x.shape[1])), jnp.broadcast_to(x - high, (8, x.shape[1]))]
    return jnp.concatenate(both, axis=0).astype(BF16)


def kernel(
    source, target, slot_source, slot_target, source_id, target_id, count,
    log_source, log_target,
    units, window, kernels, row_part, listed, part, pick_window, u_rows, row_mask,
    column_out, column_in, scale_in, scale_out, tile_id,
    z_send, z_recv, p_send, p_recv, p2_send, p2_recv, q_send, q_recv, q2_send, q2_recv, d_send, d_recv,
    x_send, x_recv,
):
    z = lax.axis_index("group")
    m = lax.axis_index("member")
    x, y, core = lax.div(m, 8), lax.rem(lax.div(m, 2), 4), lax.rem(m, 2)

    def device(kind, a, b):
        c = core if kind == 0 else 1 - core
        dx = jnp.where(c == 0, a, b)
        dy = jnp.where(c == 0, b, a)
        return (lax.rem(x + dx, 4) * 4 + lax.rem(y + dy, 4)) * 2 + c

    z_next, z_last = lax.rem(z + 1, 8), lax.rem(z + 7, 8)
    p_next, p_last = (z, device(0, 1, 0)), (z, device(0, 3, 0))
    q_next, q_last = (z, device(0, 0, 1)), (z, device(0, 0, 3))
    sibling = (z, device(1, 0, 0))

    barrier = pltpu.get_barrier_semaphore()
    neighbours = (p_next, p_last, q_next, q_last, sibling, (z_next, m), (z_last, m))
    for neighbour in neighbours:
        pl.semaphore_signal(barrier, inc=1, device_id=neighbour, device_id_type=MESH)
    window[place(0, 0, 0)] = unit(target[...])
    pl.semaphore_wait(barrier, len(neighbours))

    def copy(src, dst, send, recv, to):
        return pltpu.make_async_remote_copy(
            src_ref=src, dst_ref=dst, send_sem=send, recv_sem=recv, device_id=to, device_id_type=MESH
        )

    half = TILE // 2

    def z_copy():
        return copy(window.at[place(0, 0, 0)], window.at[place(BLOCK[1, 0], 0, 0)], z_send, z_recv, (z_last, m))

    def p_copy(r, way):
        src, dst = place(BLOCK[r, 0], 0, 0), place(BLOCK[r, 3 if way == 0 else 1], 0, 0)
        return copy(window.at[src], window.at[dst], p_send.at[r, way], p_recv.at[r, way], p_next if way == 0 else p_last)

    def p2_copy(r, way):
        src, dst = place(BLOCK[r, 3 if way == 0 else 1], 0, 0), place(BLOCK[r, 2], 0, 0)
        rows = pl.ds(way * half, half)
        return copy(
            window.at[src, rows], window.at[dst, rows], p2_send.at[r, way], p2_recv.at[r, way],
            p_next if way == 0 else p_last,
        )

    def q_copy(i, way):
        src, dst = place(i, 0, 0), place(i, 0, 3 if way == 0 else 1)
        return copy(window.at[src], window.at[dst], q_send.at[i, way], q_recv.at[i, way], q_next if way == 0 else q_last)

    def q2_copy(i, way):
        src, dst = place(i, 0, 3 if way == 0 else 1), place(i, 0, 2)
        rows = pl.ds(way * half, half)
        return copy(
            window.at[src, rows], window.at[dst, rows], q2_send.at[i, way], q2_recv.at[i, way],
            q_next if way == 0 else q_last,
        )

    def d_copy(i, b):
        return copy(
            window.at[place(i, 0, b)], window.at[place(i, 1, b)], d_send.at[i, b], d_recv.at[i, b], sibling
        )

    def spread(i):
        q_copy(i, 0).start()
        q_copy(i, 1).start()
        d_copy(i, 0).start()

    z_copy().start()
    p_copy(0, 0).start()
    p_copy(0, 1).start()
    spread(0)

    @pl.loop(0, SOURCES)
    def _(s):
        rows = pl.ds(pl.multiple_of(s * TILE, TILE), TILE)
        units[rows, :] = unit(source[rows, :])

    def window_place(w):
        r, x_to, y_to, core_to = w >> 5, (w >> 3) & 3, (w >> 1) & 3, w & 1
        dx, dy = (x_to - x + 4) & 3, (y_to - y + 4) & 3
        a = jnp.where(core_to == 0, dx, dy)
        b = jnp.where(core_to == 0, dy, dx)
        kind = jnp.where(core_to == core, 0, 1)
        block = jnp.zeros_like(a)
        for (r_, a_), i in BLOCK.items():
            block = jnp.where((r == r_) & (a == a_), i, block)
        return block * 8 + kind * 4 + b

    @pl.loop(0, SLOTS)
    def _(k):
        tile_id[k] = window_place(target_id[0, k]) * SOURCES + source_id[0, k]

    slot = lax.broadcasted_iota(jnp.int32, (1, SLOTS), 1)
    keep = (slot < count[0]).astype(F32)
    places = window_place(slot_target[...])
    tile_row = lax.broadcasted_iota(jnp.int32, (WINDOW, SLOTS), 0)
    window_pick = jnp.where(tile_row == places, keep, 0.0)
    pick_window[...] = window_pick.astype(BF16)
    source_row = lax.broadcasted_iota(jnp.int32, (8, SLOTS), 0)
    source_pick = jnp.where(source_row == slot_source[...], 1.0, 0.0)
    both = (window_pick[:, None, :] * source_pick[None, :, :]).reshape(WINDOW * 8, SLOTS).astype(BF16)
    listed[...] = lax.dot_general(
        both, jnp.ones((SLOTS, 128), BF16), ROWS_BY_COLUMNS, preferred_element_type=F32
    ).reshape(WINDOW, 8, 128)
    mask_row = lax.broadcasted_iota(jnp.int32, (16, TILE), 0)
    for j in range(8):
        row_mask[j] = ((mask_row == j) | (mask_row == j + 8)).astype(F32).astype(BF16)
    row_part[...] = jnp.zeros_like(row_part)

    def make(tiles):
        for s in range(SOURCES):
            rows = pl.ds(s * TILE, TILE)
            total = row_part[rows, :]
            for n in tiles:
                logits = lax.dot_general(units[rows, :], window[n], ROWS_BY_ROWS, preferred_element_type=F32)
                rounded = jnp.exp2(logits * SHARPNESS).astype(BF16)
                kernels[n * SOURCES + s] = rounded
                wide = rounded.astype(F32)
                total += (wide[:, :128] + wide[:, 128:]) * listed[n, s : s + 1, :]
            row_part[rows, :] = total

    def p_arrived(r, way):
        p_copy(r, way).wait_recv()
        p2_copy(r, way).start()
        spread(BLOCK[r, 3 if way == 0 else 1])

    def p2_arrived(r):
        p2_copy(r, 0).wait_recv()
        p2_copy(r, 1).wait_recv()
        spread(BLOCK[r, 2])

    p_arrived(0, 1)
    p_arrived(0, 0)
    z_copy().wait_recv()
    p_copy(1, 0).start()
    p_copy(1, 1).start()
    spread(BLOCK[1, 0])

    @pl.loop(0, 10)
    def _(i):
        @pl.when(i == 1)
        def _():
            p2_arrived(0)

        @pl.when(i == 2)
        def _():
            p_arrived(1, 1)
            p_arrived(1, 0)

        @pl.when(i == 4)
        def _():
            p2_arrived(1)

        @pl.when(i < 8)
        def _():
            q_copy(i, 0).wait_recv()
            q2_copy(i, 0).start()
            d_copy(i, 3).start()
            q_copy(i, 1).wait_recv()
            q2_copy(i, 1).start()
            d_copy(i, 1).start()
            make([place(i, 0, 0), place(i, 0, 1), place(i, 0, 3)])

        @pl.when((i > 0) & (i < 9))
        def _():
            j = i - 1
            q2_copy(j, 0).wait_recv()
            q2_copy(j, 1).wait_recv()
            d_copy(j, 2).start()
            d_copy(j, 0).wait_recv()
            d_copy(j, 3).wait_recv()
            d_copy(j, 1).wait_recv()
            make([place(j, 0, 2), place(j, 1, 0), place(j, 1, 1), place(j, 1, 3)])

        @pl.when(i > 1)
        def _():
            j = i - 2
            d_copy(j, 2).wait_recv()
            make([place(j, 1, 2)])

    def set_source_scale(row_sums):
        for s in range(SOURCES):
            u_rows[s] = stacked(1.0 / row_sums[s])

    def column_sweep():
        @pl.loop(0, SLOTS // 8, unroll=2)
        def _(i):
            total = jnp.zeros((16, TILE), F32)
            for j in range(8):
                k = i * 8 + j
                total += lax.dot_general(
                    u_rows[source_id[0, k]] * row_mask[j], kernels[tile_id[k]], ROWS_BY_COLUMNS,
                    preferred_element_type=F32,
                )
            part[pl.ds(pl.multiple_of(i * 8, 8), 8), :] = total[:8] + total[8:]

    def row_sweep():
        @pl.loop(0, SLOTS // 8, unroll=2)
        def _(i):
            total = jnp.zeros((16, TILE), F32)
            for j in range(8):
                k = i * 8 + j
                total += lax.dot_general(
                    stacked(scale_in[tile_id[k] >> 2]) * row_mask[j], kernels[tile_id[k]], ROWS_BY_ROWS,
                    preferred_element_type=F32,
                )
            part[pl.ds(pl.multiple_of(i * 8, 8), 8), :] = total[:8] + total[8:]

    def gathered(picks):
        high, low = high_low(part[...])
        return lax.dot_general(picks, high, ROWS_BY_COLUMNS, preferred_element_type=F32) + lax.dot_general(
            picks, low, ROWS_BY_COLUMNS, preferred_element_type=F32
        )

    def everyone():
        for i, (r, a) in enumerate(ORDER):
            for kind in range(2):
                for b in range(4):
                    n = place(i, kind, b)
                    there = (-a % 4, -b % 4) if kind == 0 else (-b % 4, -a % 4)
                    if n:
                        yield n, r, device(kind, a, b), place(BLOCK[r, there[0]], kind, there[1])

    def all_bytes(ref, sem):
        others = ref.at[pl.ds(1, WINDOW - 1)]
        pltpu.make_async_copy(others, others, sem).wait()

    def column_totals(it):
        columns = gathered(pick_window[...])
        for n in range(WINDOW):
            column_out[it, n] = columns[n : n + 1, :]
        for n, r, member, there in everyone():
            copy(
                column_out.at[it, n], column_in.at[it, there], x_send.at[it], x_recv.at[it],
                (z if r == 0 else z_next, member),
            ).start()
        all_bytes(column_in.at[it], x_recv.at[it])
        return jnp.sum(column_in[it, pl.ds(1, WINDOW - 1)], axis=0) + columns[:1, :]

    high, low = high_low(row_part[...])
    ones = jnp.ones((16, 128), BF16)
    sums = lax.dot_general(ones, high, ROWS_BY_ROWS, preferred_element_type=F32) + lax.dot_general(
        ones, low, ROWS_BY_ROWS, preferred_element_type=F32
    )
    set_source_scale([sums[:1, s * TILE : (s + 1) * TILE] for s in range(SOURCES)])
    column_sweep()
    scale = float(SOURCES) / column_totals(0)
    scale_out[...] = scale
    scale_in[0] = scale
    for n, r, member, there in everyone():
        copy(scale_out, scale_in.at[there], x_send.at[2], x_recv.at[2], (z if r == 0 else z_last, member)).start()
    all_bytes(scale_in, x_recv.at[2])

    row_sweep()
    source_row = lax.broadcasted_iota(jnp.int32, (16, SLOTS), 0)
    picks = jnp.where(source_row == slot_source[...], keep, 0.0).astype(BF16)
    sums = gathered(picks)
    set_source_scale([sums[s : s + 1, :] for s in range(SOURCES)])
    log_source[...] = jnp.log(float(TILE) / sums[:SOURCES, :])
    column_sweep()
    log_target[...] = jnp.log(float(SOURCES) / column_totals(1))

    z_copy().wait_send()
    for way in range(2):
        for r in range(2):
            p_copy(r, way).wait_send()
            p2_copy(r, way).wait_send()

    @pl.loop(0, 8)
    def _(i):
        for way in range(2):
            q_copy(i, way).wait_send()
            q2_copy(i, way).wait_send()
        for b in range(4):
            d_copy(i, b).wait_send()

    all_bytes(column_in.at[0], x_send.at[0])
    all_bytes(column_in.at[1], x_send.at[1])
    all_bytes(scale_in, x_send.at[2])


def shards(source, target, pair_source, pair_target, pair_count):
    vmem, smem = pl.BlockSpec(memory_space=pltpu.VMEM), pl.BlockSpec(memory_space=pltpu.SMEM)
    dma = pltpu.SemaphoreType.DMA
    log_source, log_target = pl.pallas_call(
        kernel,
        out_shape=(
            jax.ShapeDtypeStruct((SOURCES, TILE), F32),
            jax.ShapeDtypeStruct((1, TILE), F32),
        ),
        in_specs=[vmem, vmem, vmem, vmem, smem, smem, smem],
        out_specs=(vmem, vmem),
        scratch_shapes=[
            pltpu.VMEM((SOURCES * TILE, TILE), BF16),
            pltpu.VMEM((WINDOW, TILE, TILE), BF16),
            pltpu.VMEM((WINDOW * SOURCES, TILE, TILE), BF16),
            pltpu.VMEM((SOURCES * TILE, 128), F32),
            pltpu.VMEM((WINDOW, 8, 128), F32),
            pltpu.VMEM((SLOTS, TILE), F32),
            pltpu.VMEM((WINDOW, SLOTS), BF16),
            pltpu.VMEM((SOURCES, 16, TILE), BF16),
            pltpu.VMEM((8, 16, TILE), BF16),
            pltpu.VMEM((2, WINDOW, 1, TILE), F32),
            pltpu.VMEM((2, WINDOW, 1, TILE), F32),
            pltpu.VMEM((WINDOW, 1, TILE), F32),
            pltpu.VMEM((1, TILE), F32),
            pltpu.SMEM((SLOTS,), jnp.int32),
            dma, dma,
            dma((2, 2)), dma((2, 2)),
            dma((2, 2)), dma((2, 2)),
            dma((8, 2)), dma((8, 2)),
            dma((8, 2)), dma((8, 2)),
            dma((8, 4)), dma((8, 4)),
            dma((3,)), dma((3,)),
        ],
        compiler_params=pltpu.CompilerParams(
            collective_id=0, has_side_effects=True, vmem_limit_bytes=60 * 2**20
        ),
    )(source, target, pair_source, pair_target, pair_source, pair_target, pair_count)
    return log_source.reshape(SOURCES * TILE), log_target.reshape(TILE)


def solution(mesh):
    placed = (
        P(("group", "member"), None),
        P(("group", "member"), None),
        P(("group", "member"), None),
        P(("group", "member"), None),
        P(("group", "member")),
    )
    return jax.shard_map(
        shards,
        mesh=mesh,
        in_specs=placed,
        out_specs=(P(("group", "member")), P(("group", "member"))),
        check_vma=False,
    )
```

time: 409 us -> 85 us (0.21)
  other arithmetic: 101 us -> 0 us
  local copies, waits for them, and re-layouts: 91.8 us -> 2.46 us
  Pallas kernels: 0 us -> 81.1 us
  waiting for transfers between devices: 61.8 us -> 0 us
  loops' own time: 59.9 us -> 0 us
  blocking collectives: 36.3 us -> 0 us
  matrix products: 31.2 us -> 0 us
  between operations: 14.9 us -> 1.3 us
  starting transfers between devices: 9.9 us -> 0 us
    pallas_call x0 -> x1, Pallas kernels: none -> 81.1 us  [shards(): pl.pallas_call(kernel, out_shape=(jax.ShapeDtypeStruct((SOURCES, TILE), F...]
    reduce_sum x36 -> x0, other arithmetic: 68.9 us -> none  [the longest x16 35.4 us: row_block(): jnp.sum(boltzmann_factor_patches.astype(jnp.float32) * weights[:, None, :...]
    gather x48 -> x0, local copies, waits for them, and re-layouts: 67.5 us -> none  [the longest x8 43.6 us: kernels(): partners = window[frame_labels]]
    another operation x5 -> x0, loops' own time: 59.9 us -> none  [the longest x2 31.9 us: shards(): lax.map(column_block, block_inputs).reshape(slot_count, cells_per_tile)]
    all_gather x1 -> x0, waiting for transfers between devices: 52.6 us -> none  [in_one_piece(): result = lax.all_gather(both, axis, axis=dim, tiled=True)]
    all_to_all x3 -> x0, blocking collectives: 36.3 us -> none  [the longest x2 24.6 us: sum_at_owner(): lax.all_to_all(pieces, axis, split_axis=0, concat_axis=0, tiled=True)]
    dot_general x12 -> x0, matrix products: 31.2 us -> none  [the longest x8 30.1 us: kernels(): jnp.einsum('pid,pjd->pij', own_rows, partners, preferred_element_type=jnp...]
    concatenate x3 -> x0, other arithmetic: 25.6 us -> none  [the longest x1 24.8 us: shards(): jnp.concatenate([own_window, next_window], 0)]
  transfers between devices with their start and end apart: 5 -> 0, of which waited for: 5 -> 0; matrix products, arithmetic and copies ran while one was open for 2% -> 0% of each run, Pallas kernels for 0% -> 0%
where the time goes in v1:
time: 85 us; the launch traced here: 84.8 us
  Pallas kernels  81.1 us (95%)
  local copies, waits for them, and re-layouts  2.46 us (3%)
  between operations  1.3 us (2%)
    pallas_call x1, Pallas kernels, shards(): pl.pallas_call(kernel, out_shape=(jax.ShapeDtypeStruct((SOURCES, TILE), F...  81.1 us
    unnamed x6, local copies, waits for them, and re-layouts  2.46 us

profile of v1, /device:TPU:1, one launch (start us, length us, event | category | flops | bytes accessed | tf_op | source)
XLA Modules:
  0.0 84.8 jit_solution(10148867078300572259)
XLA Ops:
  1.3 81.1 %shard_map.68 = (f32[4,256]{1,0:T(4,128)}, f32[1,256]{1,0:T(1,128)}) custom-call(bf16[1024,256]{1,0:T(8,128)(2,1)} %source.1, bf16[256,256]{1,0:T(8,128)(2,1)} %target.1, s32[1,128]{1,0:T(1,128)} %source_id.1, s32[1,128]{1,0:T(1,128)} %target_id.1, s32[1,128]{1,0:T(1,128)} %source_id.1, s32[1,128]{1,0:T(1,128)} %target_id.1, s32[1]{0:T(128)S(6)} %copy.9.count), custom_call_target="tpu_custom_call" | custom-call | tf_op jit(solution)/shard_map/pallas_call | solution.py:332
  82.4 0.0 copy-start
  82.4 0.7 copy-done
  83.0 0.6 copy.7
  83.6 0.0 copy-start.1
  83.6 0.6 copy-done.1
  84.3 0.6 copy.10
Async XLA Ops:
  82.4 0.7 copy-start
  83.6 0.6 copy-start.1

commit v2 on v1

v2 whole, which is shorter than its diff:
```python
import jax
import jax.numpy as jnp
from jax import lax
from jax.experimental import pallas as pl
from jax.experimental.pallas import tpu as pltpu
from jax.sharding import PartitionSpec as P

MESH = pl.DeviceIdType.MESH
F32, BF16 = jnp.float32, jnp.bfloat16
ROWS_BY_ROWS = (((1,), (1,)), ((), ()))
ROWS_BY_COLUMNS = (((1,), (0,)), ((), ()))
SHARPNESS = 20.0 * 1.4426950408889634
TILE = 256
SOURCES = 4
WINDOW = 64
SLOTS = 128
ARRIVAL = (
    0, 10, 30, 1000, 100, 3, 1, 20, 110, 130, 1100, 13, 11, 33, 31, 103,
    101, 120, 2, 1010, 1030, 113, 111, 133, 131, 12, 32, 102, 1110, 1130, 23, 21,
    1020, 1003, 1001, 112, 132, 22, 123, 121, 1120, 1013, 1011, 1103, 1101, 1033, 1031, 122,
    1002, 1012, 1032, 1113, 1111, 1133, 1131, 1023, 1021, 1102, 1112, 1132, 1022, 1123, 1121, 1122,
)
PLACE = {(t // 1000, t // 100 % 10, t // 10 % 10, t % 10): n for n, t in enumerate(ARRIVAL)}
GROUP = 8
UNROLL = 16


def place(r, kind, a, b):
    return PLACE[r, kind, a % 4, b % 4]


def unit(values):
    floats = values.astype(F32)
    return (floats * lax.rsqrt(jnp.sum(floats * floats, axis=1, keepdims=True) + 1e-06)).astype(BF16)


def high_low(x):
    high = x.astype(BF16)
    return high, (x - high.astype(F32)).astype(BF16)


def stacked(x):
    high = x.astype(BF16).astype(F32)
    both = [jnp.broadcast_to(high, (8, x.shape[1])), jnp.broadcast_to(x - high, (8, x.shape[1]))]
    return jnp.concatenate(both, axis=0).astype(BF16)


def kernel(
    source, target, slot_source, slot_target, source_id, count,
    row_sums, column_sums,
    units, window, kernels, turned, row_part, listed, part, pick_window, u_rows, row_mask,
    column_out, column_in, scale_in, scale_out, tile_row_id, tile_id, local,
    t_send, t_recv, d_send, d_recv,
    x_send, x_recv,
):
    z = lax.axis_index("group")
    m = lax.axis_index("member")
    x, y, core = lax.div(m, 8), lax.rem(lax.div(m, 2), 4), lax.rem(m, 2)

    def device(kind, a, b):
        c = core if kind == 0 else 1 - core
        dx = jnp.where(c == 0, a, b)
        dy = jnp.where(c == 0, b, a)
        return (lax.rem(x + dx, 4) * 4 + lax.rem(y + dy, 4)) * 2 + c

    z_next, z_last = lax.rem(z + 1, 8), lax.rem(z + 7, 8)
    sibling = (z, device(1, 0, 0))
    devices = {
        "p+": (z, device(0, 1, 0)), "p-": (z, device(0, 3, 0)), "q+": (z, device(0, 0, 1)), "q-": (z, device(0, 0, 3)),
        "z-": (z_last, m),
    }

    barrier = pltpu.get_barrier_semaphore()
    neighbours = (*devices.values(), (z_next, m), sibling)
    for neighbour in neighbours:
        pl.semaphore_signal(barrier, inc=1, device_id=neighbour, device_id_type=MESH)
    window[0] = unit(target[...])
    pl.semaphore_wait(barrier, len(neighbours))

    def copy(src, dst, send, recv, to):
        return pltpu.make_async_remote_copy(
            src_ref=src, dst_ref=dst, send_sem=send, recv_sem=recv, device_id=to, device_id_type=MESH
        )

    half = TILE // 2
    sends = []

    def tile_copy(src, dst, to, rows=None):
        key = (src, dst, to, rows)
        if key not in sends:
            sends.append(key)
        i = sends.index(key)
        at = pl.ds(0, TILE) if rows is None else pl.ds(rows * half, half)
        return copy(window.at[place(*src), at], window.at[place(*dst), at], t_send.at[i], t_recv.at[i], devices[to])

    def p(r, way):
        return tile_copy((r, 0, 0, 0), (r, 0, 3 if way == 0 else 1, 0), "p+" if way == 0 else "p-")

    def p2(way):
        return tile_copy((0, 0, 3 if way == 0 else 1, 0), (0, 0, 2, 0), "p+" if way == 0 else "p-", way)

    def q(r, a, way):
        return tile_copy((r, 0, a, 0), (r, 0, a, 3 if way == 0 else 1), "q+" if way == 0 else "q-")

    def q2(a, way):
        return tile_copy((0, 0, a, 3 if way == 0 else 1), (0, 0, a, 2), "q+" if way == 0 else "q-", way)

    def down(a, b):
        return tile_copy((0, 0, a, b), (1, 0, a, b), "z-")

    def across(r, a, b):
        n = place(r, 0, a, b)
        return copy(window.at[n], window.at[place(r, 1, a, b)], d_send.at[n], d_recv.at[n], sibling)

    def spread(r, a):
        q(r, a, 0).start()
        q(r, a, 1).start()
        across(r, a, 0).start()

    p(0, 0).start()
    p(0, 1).start()
    down(0, 0).start()
    spread(0, 0)

    @pl.loop(0, SOURCES)
    def _(s):
        rows = pl.ds(pl.multiple_of(s * TILE, TILE), TILE)
        units[s] = unit(source[rows, :])

    slots = slot_target[...]
    r, x_to, y_to, core_to = slots >> 5, (slots >> 3) & 3, (slots >> 1) & 3, slots & 1
    dx, dy = (x_to - x + 4) & 3, (y_to - y + 4) & 3
    code = r * 32 + jnp.where(core_to == core, 0, 16) + jnp.where(core_to == 0, dx * 4 + dy, dy * 4 + dx)
    places = jnp.zeros_like(code)
    for (r_, kind, a, b), n in PLACE.items():
        places = jnp.where(code == r_ * 32 + kind * 16 + a * 4 + b, n, places)
    tile_row_id[...] = places * SOURCES + slot_source[...]
    table = pltpu.make_async_copy(tile_row_id, tile_id, local)
    table.start()

    slot = lax.broadcasted_iota(jnp.int32, (1, SLOTS), 1)
    keep = (slot < count[0]).astype(F32)
    tile_row = lax.broadcasted_iota(jnp.int32, (WINDOW, SLOTS), 0)
    window_pick = jnp.where(tile_row == places, keep, 0.0)
    pick_window[...] = window_pick.astype(BF16)
    source_row = lax.broadcasted_iota(jnp.int32, (8, SLOTS), 0)
    source_pick = jnp.where(source_row == slot_source[...], 1.0, 0.0)
    both = (window_pick[:, None, :] * source_pick[None, :, :]).reshape(WINDOW * 8, SLOTS).astype(BF16)
    listed[...] = lax.dot_general(
        both, jnp.ones((SLOTS, 128), BF16), ROWS_BY_COLUMNS, preferred_element_type=F32
    ).reshape(WINDOW, 8, 128)
    mask_row = lax.broadcasted_iota(jnp.int32, (16, TILE), 0)
    for j in range(8):
        row_mask[j] = ((mask_row == j) | (mask_row == j + 8)).astype(F32).astype(BF16)
    row_part[...] = jnp.zeros_like(row_part)

    def make(tiles):
        for s in range(SOURCES):
            rows = pl.ds(s * TILE, TILE)
            total = row_part[rows, :]
            for n in tiles:
                logits = lax.dot_general(units[s], window[n], ROWS_BY_ROWS, preferred_element_type=F32)
                rounded = jnp.exp2(logits * SHARPNESS).astype(BF16)
                kernels[n * SOURCES + s] = rounded
                wide = rounded.astype(F32)
                total += (wide[:, :128] + wide[:, 128:]) * listed[n, s : s + 1, :]
            row_part[rows, :] = total

    arrivals = {}

    def event(*tiles):
        def put(act):
            arrivals[tiles] = act
        return put

    for way in range(2):
        @event((0, 0, 3 if way == 0 else 1, 0))
        def _(way=way):
            p(0, way).wait_recv()
            p2(way).start()
            spread(0, 3 if way == 0 else 1)

        @event((1, 0, 3 if way == 0 else 1, 0))
        def _(way=way):
            p(1, way).wait_recv()
            spread(1, 3 if way == 0 else 1)

        for a in range(4):
            @event((0, 0, a, 3 if way == 0 else 1))
            def _(a=a, way=way):
                q(0, a, way).wait_recv()
                q2(a, way).start()
                across(0, a, 3 if way == 0 else 1).start()

            @event((1, 0, a, 3 if way == 0 else 1))
            def _(a=a, way=way):
                q(1, a, way).wait_recv()
                across(1, a, 3 if way == 0 else 1).start()

    @event((1, 0, 0, 0))
    def _():
        down(0, 0).wait_recv()
        p(1, 0).start()
        p(1, 1).start()
        spread(1, 0)

    @event((0, 0, 2, 0))
    def _():
        p2(0).wait_recv()
        p2(1).wait_recv()
        down(2, 0).start()
        spread(0, 2)

    @event((1, 0, 2, 0))
    def _():
        down(2, 0).wait_recv()
        spread(1, 2)

    for a in range(4):
        @event((0, 0, a, 2))
        def _(a=a):
            q2(a, 0).wait_recv()
            q2(a, 1).wait_recv()
            down(a, 2).start()
            across(0, a, 2).start()

        @event((1, 0, a, 2))
        def _(a=a):
            down(a, 2).wait_recv()
            across(1, a, 2).start()

        for r in range(2):
            for b in range(4):
                @event((r, 1, a, b))
                def _(r=r, a=a, b=b):
                    across(r, a, b).wait_recv()

    acts = {PLACE[tile]: act for (tile,), act in arrivals.items()}

    @pl.loop(0, WINDOW // GROUP)
    def _(i):
        for step in range(WINDOW // GROUP):
            @pl.when(i == step)
            def _(step=step):
                for n in range(step * GROUP, (step + 1) * GROUP):
                    if n:
                        acts[n]()

        make([i * GROUP + t for t in range(GROUP)])

    table.wait()

    def set_source_scale(row_sums):
        for s in range(SOURCES):
            u_rows[s] = stacked(1.0 / row_sums[s])

    def column_sweep():
        @pl.loop(0, SLOTS // 8, unroll=UNROLL)
        def _(i):
            total = jnp.zeros((16, TILE), F32)
            for j in range(8):
                k = i * 8 + j
                total += lax.dot_general(
                    u_rows[source_id[0, k]] * row_mask[j], kernels[tile_id[0, k]], ROWS_BY_COLUMNS,
                    preferred_element_type=F32,
                )
            part[pl.ds(pl.multiple_of(i * 8, 8), 8), :] = total[:8] + total[8:]

    def turn(first):
        @pl.loop(0, SLOTS // 2, unroll=8)
        def _(k):
            k = first + k
            logits = lax.dot_general(
                window[tile_id[0, k] >> 2], units[source_id[0, k]], ROWS_BY_ROWS, preferred_element_type=F32
            )
            turned[k] = jnp.exp2(logits * SHARPNESS).astype(BF16)

    def row_sweep():
        @pl.loop(0, SLOTS // 8, unroll=UNROLL)
        def _(i):
            total = jnp.zeros((16, TILE), F32)
            for j in range(8):
                k = i * 8 + j
                total += lax.dot_general(
                    stacked(scale_in[tile_id[0, k] >> 2]) * row_mask[j], turned[k], ROWS_BY_COLUMNS,
                    preferred_element_type=F32,
                )
            part[pl.ds(pl.multiple_of(i * 8, 8), 8), :] = total[:8] + total[8:]

    def gathered(picks):
        high, low = high_low(part[...])
        return lax.dot_general(picks, high, ROWS_BY_COLUMNS, preferred_element_type=F32) + lax.dot_general(
            picks, low, ROWS_BY_COLUMNS, preferred_element_type=F32
        )

    def everyone():
        for (r, kind, a, b), n in PLACE.items():
            there = (-a, -b) if kind == 0 else (-b, -a)
            if n:
                yield n, r, device(kind, a, b), place(r, kind, *there)

    def all_bytes(ref, sem):
        others = ref.at[pl.ds(1, WINDOW - 1)]
        pltpu.make_async_copy(others, others, sem).wait()

    def column_totals(it):
        columns = gathered(pick_window[...])
        for n in range(WINDOW):
            column_out[it, n] = columns[n : n + 1, :]
        for n, r, member, there in everyone():
            copy(
                column_out.at[it, n], column_in.at[it, there], x_send.at[it], x_recv.at[it],
                (z if r == 0 else z_next, member),
            ).start()
        if it == 0:
            turn(0)
        all_bytes(column_in.at[it], x_recv.at[it])
        return jnp.sum(column_in[it, pl.ds(1, WINDOW - 1)], axis=0) + columns[:1, :]

    high, low = high_low(row_part[...])
    ones = jnp.ones((16, 128), BF16)
    sums = lax.dot_general(ones, high, ROWS_BY_ROWS, preferred_element_type=F32) + lax.dot_general(
        ones, low, ROWS_BY_ROWS, preferred_element_type=F32
    )
    set_source_scale([sums[:1, s * TILE : (s + 1) * TILE] for s in range(SOURCES)])
    column_sweep()
    scale = float(SOURCES) / column_totals(0)
    scale_out[...] = scale
    scale_in[0] = scale
    for n, r, member, there in everyone():
        copy(scale_out, scale_in.at[there], x_send.at[2], x_recv.at[2], (z if r == 0 else z_last, member)).start()
    turn(SLOTS // 2)
    all_bytes(scale_in, x_recv.at[2])

    row_sweep()
    source_row = lax.broadcasted_iota(jnp.int32, (16, SLOTS), 0)
    picks = jnp.where(source_row == slot_source[...], keep, 0.0).astype(BF16)
    sums = gathered(picks)
    set_source_scale([sums[s : s + 1, :] for s in range(SOURCES)])
    for s in range(SOURCES):
        for h in range(2):
            row_sums[pl.ds(2 * s + h, 1), :] = sums[s : s + 1, h * 128 : (h + 1) * 128]
    column_sweep()
    totals = column_totals(1)
    for h in range(2):
        column_sums[pl.ds(h, 1), :] = totals[:, h * 128 : (h + 1) * 128]

    for key in list(sends):
        tile_copy(*key).wait_send()
    for r in range(2):
        for a in range(4):
            for b in range(4):
                across(r, a, b).wait_send()
    all_bytes(column_in.at[0], x_send.at[0])
    all_bytes(column_in.at[1], x_send.at[1])
    all_bytes(scale_in, x_send.at[2])


def shards(source, target, pair_source, pair_target, pair_count):
    vmem, smem = pl.BlockSpec(memory_space=pltpu.VMEM), pl.BlockSpec(memory_space=pltpu.SMEM)
    dma = pltpu.SemaphoreType.DMA
    row_sums, column_sums = pl.pallas_call(
        kernel,
        out_shape=(
            jax.ShapeDtypeStruct((8, 128), F32),
            jax.ShapeDtypeStruct((2, 128), F32),
        ),
        in_specs=[vmem, vmem, vmem, vmem, smem, smem],
        out_specs=(vmem, vmem),
        scratch_shapes=[
            pltpu.VMEM((SOURCES, TILE, TILE), BF16),
            pltpu.VMEM((WINDOW, TILE, TILE), BF16),
            pltpu.VMEM((WINDOW * SOURCES, TILE, TILE), BF16),
            pltpu.VMEM((SLOTS, TILE, TILE), BF16),
            pltpu.VMEM((SOURCES * TILE, 128), F32),
            pltpu.VMEM((WINDOW, 8, 128), F32),
            pltpu.VMEM((SLOTS, TILE), F32),
            pltpu.VMEM((WINDOW, SLOTS), BF16),
            pltpu.VMEM((SOURCES, 16, TILE), BF16),
            pltpu.VMEM((8, 16, TILE), BF16),
            pltpu.VMEM((2, WINDOW, 1, TILE), F32),
            pltpu.VMEM((2, WINDOW, 1, TILE), F32),
            pltpu.VMEM((WINDOW, 1, TILE), F32),
            pltpu.VMEM((1, TILE), F32),
            pltpu.VMEM((1, SLOTS), jnp.int32),
            pltpu.SMEM((1, SLOTS), jnp.int32),
            dma,
            dma((40,)), dma((40,)),
            dma((WINDOW,)), dma((WINDOW,)),
            dma((3,)), dma((3,)),
        ],
        compiler_params=pltpu.CompilerParams(
            collective_id=0, has_side_effects=True, vmem_limit_bytes=62 * 2**20
        ),
    )(source, target, pair_source, pair_target, pair_source, pair_count)
    return jnp.log(float(TILE) / row_sums.reshape(SOURCES * TILE)), jnp.log(float(SOURCES) / column_sums.reshape(TILE))


def solution(mesh):
    placed = (
        P(("group", "member"), None),
        P(("group", "member"), None),
        P(("group", "member"), None),
        P(("group", "member"), None),
        P(("group", "member")),
    )
    return jax.shard_map(
        shards,
        mesh=mesh,
        in_specs=placed,
        out_specs=(P(("group", "member")), P(("group", "member"))),
        check_vma=False,
    )
```

time: 85 us -> 71.9 us (0.85)
  Pallas kernels: 81.1 us -> 68.6 us
  local copies, waits for them, and re-layouts: 2.46 us -> 0.01 us
  other arithmetic: 0 us -> 1.86 us
    pallas_call x1, Pallas kernels: 81.1 us -> 68.6 us  [shards(): pl.pallas_call(kernel, out_shape=(jax.ShapeDtypeStruct((8, 128), F32), ja...]
    unnamed x6 -> x2, local copies, waits for them, and re-layouts: 2.46 us -> 0.01 us
    log x0 -> x2, other arithmetic: none -> 1.86 us  [the longest x1 1.28 us: shards(): jnp.log(float(TILE) / row_sums.reshape(SOURCES * TILE))]
where the time goes in v2:
time: 71.9 us; the launch traced here: 71.8 us
  Pallas kernels  68.6 us (95%)
  other arithmetic  1.86 us (3%)
  between operations  1.29 us (2%)
    pallas_call x1, Pallas kernels, shards(): pl.pallas_call(kernel, out_shape=(jax.ShapeDtypeStruct((8, 128), F32), ja...  68.6 us

profile of v2, /device:TPU:1, one launch (start us, length us, event | category | flops | bytes accessed | tf_op | source)
XLA Modules:
  0.0 71.8 jit_solution(3781082348600702685)
XLA Ops:
  1.3 68.6 %shard_map.68 = (f32[8,128]{1,0:T(8,128)}, f32[2,128]{1,0:T(2,128)}) custom-call(bf16[1024,256]{1,0:T(8,128)(2,1)} %source.1, bf16[256,256]{1,0:T(8,128)(2,1)} %target.1, s32[1,128]{1,0:T(1,128)} %source_id.1, s32[1,128]{1,0:T(1,128)} %slot_target.1, s32[1,128]{1,0:T(1,128)} %source_id.1, s32[1]{0:T(128)S(6)} %copy.7.count), custom_call_target="tpu_custom_call" | custom-call | tf_op jit(solution)/shard_map/pallas_call | solution.py:362
  69.9 0.0 copy-start
  69.9 1.3 %log_bitcast_fusion = f32[1024]{0:T(1024)} fusion(f32[8,128]{1,0:T(8,128)} %get-tuple-element.4), kind=kLoop, calls=%fused_computation | loop fusion | flops 1024 | bytes 8192 | tf_op jit(solution)/shard_map/log | solution.py:396
  71.2 0.0 copy-done
  71.2 0.6 log_bitcast_fusion.1
Async XLA Ops:
  69.9 1.3 %copy-start = (f32[2,128]{1,0:T(2,128)S(1)}, f32[2,128]{1,0:T(2,128)}, u32[]{:S(2)}) copy-start(f32[2,128]{1,0:T(2,128)} %get-tuple-element.5) | copy-start | bytes 3076

commit v3 on v2

--- a/solution.py
+++ b/solution.py
@@ -46,8 +46,9 @@
 
 
 def kernel(
-    source, target, slot_source, slot_target, source_id, count,
+    source_in, target_in, pair_source, pair_target, pair_count,
     row_sums, column_sums,
+    source, target, slot_source, slot_target, source_id, count, loads,
     units, window, kernels, turned, row_part, listed, part, pick_window, u_rows, row_mask,
     column_out, column_in, scale_in, scale_out, tile_row_id, tile_id, local,
     t_send, t_recv, d_send, d_recv,
@@ -74,6 +75,14 @@
     neighbours = (*devices.values(), (z_next, m), sibling)
     for neighbour in neighbours:
         pl.semaphore_signal(barrier, inc=1, device_id=neighbour, device_id_type=MESH)
+    inputs = (
+        (target_in, target), (source_in, source), (pair_source, source_id), (pair_source, slot_source),
+        (pair_target, slot_target), (pair_count, count),
+    )
+    inputs = [pltpu.make_async_copy(*pair, loads.at[i]) for i, pair in enumerate(inputs)]
+    for load in inputs:
+        load.start()
+    inputs[0].wait()
     window[0] = unit(target[...])
     pl.semaphore_wait(barrier, len(neighbours))
 
@@ -121,6 +130,9 @@
     p(0, 1).start()
     down(0, 0).start()
     spread(0, 0)
+
+    for load in inputs[1:]:
+        load.wait()
 
     @pl.loop(0, SOURCES)
     def _(s):
@@ -299,23 +311,37 @@
             if n:
                 yield n, r, device(kind, a, b), place(r, kind, *there)
 
-    def all_bytes(ref, sem):
-        others = ref.at[pl.ds(1, WINDOW - 1)]
+    def all_bytes(others, sem):
         pltpu.make_async_copy(others, others, sem).wait()
+
+    other_rows = pl.ds(2, 2 * WINDOW - 2)
+    other_tiles = pl.ds(1, WINDOW - 1)
+
+    def sent_tiles():
+        for key in list(sends):
+            tile_copy(*key).wait_send()
+        for r in range(2):
+            for a in range(4):
+                for b in range(4):
+                    across(r, a, b).wait_send()
 
     def column_totals(it):
         columns = gathered(pick_window[...])
-        for n in range(WINDOW):
-            column_out[it, n] = columns[n : n + 1, :]
+        for h in range(2):
+            lanes = columns[:, h * 128 : (h + 1) * 128]
+            column_out[it, pl.ds(h, WINDOW, stride=2), :] = lanes
+            column_in[it, pl.ds(h, 1), :] = lanes[:1]
         for n, r, member, there in everyone():
             copy(
-                column_out.at[it, n], column_in.at[it, there], x_send.at[it], x_recv.at[it],
+                column_out.at[it, pl.ds(2 * n, 2)], column_in.at[it, pl.ds(2 * there, 2)], x_send.at[it], x_recv.at[it],
                 (z if r == 0 else z_next, member),
             ).start()
         if it == 0:
             turn(0)
-        all_bytes(column_in.at[it], x_recv.at[it])
-        return jnp.sum(column_in[it, pl.ds(1, WINDOW - 1)], axis=0) + columns[:1, :]
+            sent_tiles()
+        all_bytes(column_in.at[it, other_rows], x_recv.at[it])
+        total = jnp.sum(column_in[it].reshape(16, 8, 128), axis=0)
+        return total[0:2] + total[2:4] + total[4:6] + total[6:8]
 
     high, low = high_low(row_part[...])
     ones = jnp.ones((16, 128), BF16)
@@ -324,13 +350,15 @@
     )
     set_source_scale([sums[:1, s * TILE : (s + 1) * TILE] for s in range(SOURCES)])
     column_sweep()
-    scale = float(SOURCES) / column_totals(0)
+    totals = float(SOURCES) / column_totals(0)
+    scale = jnp.concatenate([totals[0:1], totals[1:2]], axis=1)
     scale_out[...] = scale
     scale_in[0] = scale
     for n, r, member, there in everyone():
         copy(scale_out, scale_in.at[there], x_send.at[2], x_recv.at[2], (z if r == 0 else z_last, member)).start()
     turn(SLOTS // 2)
-    all_bytes(scale_in, x_recv.at[2])
+    all_bytes(column_in.at[0, other_rows], x_send.at[0])
+    all_bytes(scale_in.at[other_tiles], x_recv.at[2])
 
     row_sweep()
     source_row = lax.broadcasted_iota(jnp.int32, (16, SLOTS), 0)
@@ -341,23 +369,14 @@
         for h in range(2):
             row_sums[pl.ds(2 * s + h, 1), :] = sums[s : s + 1, h * 128 : (h + 1) * 128]
     column_sweep()
-    totals = column_totals(1)
-    for h in range(2):
-        column_sums[pl.ds(h, 1), :] = totals[:, h * 128 : (h + 1) * 128]
-
-    for key in list(sends):
-        tile_copy(*key).wait_send()
-    for r in range(2):
-        for a in range(4):
-            for b in range(4):
-                across(r, a, b).wait_send()
-    all_bytes(column_in.at[0], x_send.at[0])
-    all_bytes(column_in.at[1], x_send.at[1])
-    all_bytes(scale_in, x_send.at[2])
+    all_bytes(scale_in.at[other_tiles], x_send.at[2])
+    column_sums[...] = column_totals(1)
+
+    all_bytes(column_in.at[1, other_rows], x_send.at[1])
 
 
 def shards(source, target, pair_source, pair_target, pair_count):
-    vmem, smem = pl.BlockSpec(memory_space=pltpu.VMEM), pl.BlockSpec(memory_space=pltpu.SMEM)
+    vmem = pl.BlockSpec(memory_space=pltpu.VMEM)
     dma = pltpu.SemaphoreType.DMA
     row_sums, column_sums = pl.pallas_call(
         kernel,
@@ -365,9 +384,13 @@
             jax.ShapeDtypeStruct((8, 128), F32),
             jax.ShapeDtypeStruct((2, 128), F32),
         ),
-        in_specs=[vmem, vmem, vmem, vmem, smem, smem],
+        in_specs=[pl.BlockSpec(memory_space=pl.ANY)] * 5,
         out_specs=(vmem, vmem),
         scratch_shapes=[
+            pltpu.VMEM(source.shape, BF16), pltpu.VMEM(target.shape, BF16),
+            pltpu.VMEM((1, SLOTS), jnp.int32), pltpu.VMEM((1, SLOTS), jnp.int32),
+            pltpu.SMEM((1, SLOTS), jnp.int32), pltpu.SMEM((1,), jnp.int32),
+            dma((6,)),
             pltpu.VMEM((SOURCES, TILE, TILE), BF16),
             pltpu.VMEM((WINDOW, TILE, TILE), BF16),
             pltpu.VMEM((WINDOW * SOURCES, TILE, TILE), BF16),
@@ -378,8 +401,8 @@
             pltpu.VMEM((WINDOW, SLOTS), BF16),
             pltpu.VMEM((SOURCES, 16, TILE), BF16),
             pltpu.VMEM((8, 16, TILE), BF16),
-            pltpu.VMEM((2, WINDOW, 1, TILE), F32),
-            pltpu.VMEM((2, WINDOW, 1, TILE), F32),
+            pltpu.VMEM((2, 2 * WINDOW, 128), F32),
+            pltpu.VMEM((2, 2 * WINDOW, 128), F32),
             pltpu.VMEM((WINDOW, 1, TILE), F32),
             pltpu.VMEM((1, TILE), F32),
             pltpu.VMEM((1, SLOTS), jnp.int32),
@@ -392,7 +415,7 @@
         compiler_params=pltpu.CompilerParams(
             collective_id=0, has_side_effects=True, vmem_limit_bytes=62 * 2**20
         ),
-    )(source, target, pair_source, pair_target, pair_source, pair_count)
+    )(source, target, pair_source, pair_target, pair_count)
     return jnp.log(float(TILE) / row_sums.reshape(SOURCES * TILE)), jnp.log(float(SOURCES) / column_sums.reshape(TILE))
 
 

time: 71.9 us -> 70.7 us (0.983)
  Pallas kernels: 68.6 us -> 67.4 us
    pallas_call x1, Pallas kernels: 68.6 us -> 67.4 us  [shards(): pl.pallas_call(kernel, out_shape=(jax.ShapeDtypeStruct((8, 128), F32), ja...]
where the time goes in v3:
time: 70.7 us; the launch traced here: 70.5 us
  Pallas kernels  67.4 us (95%)
  other arithmetic  1.86 us (3%)
  between operations  1.29 us (2%)
    pallas_call x1, Pallas kernels, shards(): pl.pallas_call(kernel, out_shape=(jax.ShapeDtypeStruct((8, 128), F32), ja...  67.4 us

profile of v3, /device:TPU:1, one launch (start us, length us, event | category | flops | bytes accessed | tf_op | source)
XLA Modules:
  0.0 70.5 jit_solution(604955734813228583)
XLA Ops:
  1.3 67.4 %shard_map.68 = (f32[8,128]{1,0:T(8,128)}, f32[2,128]{1,0:T(2,128)}) custom-call(bf16[1024,256]{1,0:T(8,128)(2,1)} %source_in.1, bf16[256,256]{1,0:T(8,128)(2,1)} %target_in.1, s32[1,128]{1,0:T(1,128)} %pair_source.1, s32[1,128]{1,0:T(1,128)} %pair_target.1, s32[1]{0:T(128)S(6)} %copy.7.pair_count), custom_call_target="tpu_custom_call" | custom-call | tf_op jit(solution)/shard_map/pallas_call | solution.py:381
  68.7 0.0 copy-start
  68.7 1.3 %log_bitcast_fusion = f32[1024]{0:T(1024)} fusion(f32[8,128]{1,0:T(8,128)} %get-tuple-element.4), kind=kLoop, calls=%fused_computation | loop fusion | flops 1024 | bytes 8192 | tf_op jit(solution)/shard_map/log | solution.py:419
  69.9 0.0 copy-done
  69.9 0.6 log_bitcast_fusion.1
Async XLA Ops:
  68.7 1.3 %copy-start = (f32[2,128]{1,0:T(2,128)S(1)}, f32[2,128]{1,0:T(2,128)}, u32[]{:S(2)}) copy-start(f32[2,128]{1,0:T(2,128)} %get-tuple-element.5) | copy-start | bytes 3076

commit v4 on v3

--- a/solution.py
+++ b/solution.py
@@ -29,6 +29,10 @@
     return PLACE[r, kind, a % 4, b % 4]
 
 
+def distance(r, kind, a, b):
+    return r + 2 * kind + min(a, 4 - a) + min(b, 4 - b)
+
+
 def unit(values):
     floats = values.astype(F32)
     return (floats * lax.rsqrt(jnp.sum(floats * floats, axis=1, keepdims=True) + 1e-06)).astype(BF16)
@@ -251,13 +255,17 @@
 
     @pl.loop(0, WINDOW // GROUP)
     def _(i):
-        for step in range(WINDOW // GROUP):
-            @pl.when(i == step)
-            def _(step=step):
-                for n in range(step * GROUP, (step + 1) * GROUP):
+        def dispatch(first, last):
+            if last - first == 1:
+                for n in range(first * GROUP, last * GROUP):
                     if n:
                         acts[n]()
-
+                return
+            middle = (first + last) // 2
+            pl.when(i < middle)(lambda: dispatch(first, middle))
+            pl.when(i >= middle)(lambda: dispatch(middle, last))
+
+        dispatch(0, WINDOW // GROUP)
         make([i * GROUP + t for t in range(GROUP)])
 
     table.wait()
@@ -306,7 +314,7 @@
         )
 
     def everyone():
-        for (r, kind, a, b), n in PLACE.items():
+        for (r, kind, a, b), n in sorted(PLACE.items(), key=lambda item: -distance(*item[0])):
             there = (-a, -b) if kind == 0 else (-b, -a)
             if n:
                 yield n, r, device(kind, a, b), place(r, kind, *there)

time: 70.7 us -> 69.2 us (0.979)
  Pallas kernels: 67.4 us -> 65.9 us
    pallas_call x1, Pallas kernels: 67.4 us -> 65.9 us  [shards(): pl.pallas_call(kernel, out_shape=(jax.ShapeDtypeStruct((8, 128), F32), ja...]
where the time goes in v4:
time: 69.2 us; the launch traced here: 69.1 us
  Pallas kernels  65.9 us (95%)
  other arithmetic  1.86 us (3%)
  between operations  1.29 us (2%)
    pallas_call x1, Pallas kernels, shards(): pl.pallas_call(kernel, out_shape=(jax.ShapeDtypeStruct((8, 128), F32), ja...  65.9 us

profile of v4, /device:TPU:1, one launch (start us, length us, event | category | flops | bytes accessed | tf_op | source)
XLA Modules:
  0.0 69.1 jit_solution(5821434711499127081)
XLA Ops:
  1.3 65.9 %shard_map.68 = (f32[8,128]{1,0:T(8,128)}, f32[2,128]{1,0:T(2,128)}) custom-call(bf16[1024,256]{1,0:T(8,128)(2,1)} %source_in.1, bf16[256,256]{1,0:T(8,128)(2,1)} %target_in.1, s32[1,128]{1,0:T(1,128)} %pair_source.1, s32[1,128]{1,0:T(1,128)} %pair_target.1, s32[1]{0:T(128)S(6)} %copy.7.pair_count), custom_call_target="tpu_custom_call" | custom-call | tf_op jit(solution)/shard_map/pallas_call | solution.py:389
  67.2 0.0 copy-start
  67.2 1.3 %log_bitcast_fusion = f32[1024]{0:T(1024)} fusion(f32[8,128]{1,0:T(8,128)} %get-tuple-element.4), kind=kLoop, calls=%fused_computation | loop fusion | flops 1024 | bytes 8192 | tf_op jit(solution)/shard_map/log | solution.py:427
  68.5 0.0 copy-done
  68.5 0.6 log_bitcast_fusion.1
Async XLA Ops:
  67.2 1.3 %copy-start = (f32[2,128]{1,0:T(2,128)S(1)}, f32[2,128]{1,0:T(2,128)}, u32[]{:S(2)}) copy-start(f32[2,128]{1,0:T(2,128)} %get-tuple-element.5) | copy-start | bytes 3076

commit v5 on v4

--- a/solution.py
+++ b/solution.py
@@ -143,6 +143,95 @@
         rows = pl.ds(pl.multiple_of(s * TILE, TILE), TILE)
         units[s] = unit(source[rows, :])
 
+    row_part[...] = jnp.zeros_like(row_part)
+
+    def make(tiles):
+        for s in range(SOURCES):
+            rows = pl.ds(s * TILE, TILE)
+            total = row_part[rows, :]
+            for n in tiles:
+                logits = lax.dot_general(units[s], window[n], ROWS_BY_ROWS, preferred_element_type=F32)
+                rounded = jnp.exp2(logits * SHARPNESS).astype(BF16)
+                kernels[n * SOURCES + s] = rounded
+                wide = rounded.astype(F32)
+                total += (wide[:, :128] + wide[:, 128:]) * listed[n, s : s + 1, :]
+            row_part[rows, :] = total
+
+    arrivals = {}
+
+    def event(*tiles):
+        def put(act):
+            arrivals[tiles] = act
+        return put
+
+    for way in range(2):
+        @event((0, 0, 3 if way == 0 else 1, 0))
+        def _(way=way):
+            p(0, way).wait_recv()
+            p2(way).start()
+            spread(0, 3 if way == 0 else 1)
+
+        @event((1, 0, 3 if way == 0 else 1, 0))
+        def _(way=way):
+            p(1, way).wait_recv()
+            spread(1, 3 if way == 0 else 1)
+
+        for a in range(4):
+            @event((0, 0, a, 3 if way == 0 else 1))
+            def _(a=a, way=way):
+                q(0, a, way).wait_recv()
+                q2(a, way).start()
+                across(0, a, 3 if way == 0 else 1).start()
+
+            @event((1, 0, a, 3 if way == 0 else 1))
+            def _(a=a, way=way):
+                q(1, a, way).wait_recv()
+                across(1, a, 3 if way == 0 else 1).start()
+
+    @event((1, 0, 0, 0))
+    def _():
+        down(0, 0).wait_recv()
+        p(1, 0).start()
+        p(1, 1).start()
+        spread(1, 0)
+
+    @event((0, 0, 2, 0))
+    def _():
+        p2(0).wait_recv()
+        p2(1).wait_recv()
+        down(2, 0).start()
+        spread(0, 2)
+
+    @event((1, 0, 2, 0))
+    def _():
+        down(2, 0).wait_recv()
+        spread(1, 2)
+
+    for a in range(4):
+        @event((0, 0, a, 2))
+        def _(a=a):
+            q2(a, 0).wait_recv()
+            q2(a, 1).wait_recv()
+            down(a, 2).start()
+            across(0, a, 2).start()
+
+        @event((1, 0, a, 2))
+        def _(a=a):
+            down(a, 2).wait_recv()
+            across(1, a, 2).start()
+
+        for r in range(2):
+            for b in range(4):
+                @event((r, 1, a, b))
+                def _(r=r, a=a, b=b):
+                    across(r, a, b).wait_recv()
+
+    acts = {PLACE[tile]: act for (tile,), act in arrivals.items()}
+
+    early = 3
+    for n in range(1, early + 1):
+        acts[n]()
+
     slots = slot_target[...]
     r, x_to, y_to, core_to = slots >> 5, (slots >> 3) & 3, (slots >> 1) & 3, slots & 1
     dx, dy = (x_to - x + 4) & 3, (y_to - y + 4) & 3
@@ -168,97 +257,12 @@
     mask_row = lax.broadcasted_iota(jnp.int32, (16, TILE), 0)
     for j in range(8):
         row_mask[j] = ((mask_row == j) | (mask_row == j + 8)).astype(F32).astype(BF16)
-    row_part[...] = jnp.zeros_like(row_part)
-
-    def make(tiles):
-        for s in range(SOURCES):
-            rows = pl.ds(s * TILE, TILE)
-            total = row_part[rows, :]
-            for n in tiles:
-                logits = lax.dot_general(units[s], window[n], ROWS_BY_ROWS, preferred_element_type=F32)
-                rounded = jnp.exp2(logits * SHARPNESS).astype(BF16)
-                kernels[n * SOURCES + s] = rounded
-                wide = rounded.astype(F32)
-                total += (wide[:, :128] + wide[:, 128:]) * listed[n, s : s + 1, :]
-            row_part[rows, :] = total
-
-    arrivals = {}
-
-    def event(*tiles):
-        def put(act):
-            arrivals[tiles] = act
-        return put
-
-    for way in range(2):
-        @event((0, 0, 3 if way == 0 else 1, 0))
-        def _(way=way):
-            p(0, way).wait_recv()
-            p2(way).start()
-            spread(0, 3 if way == 0 else 1)
-
-        @event((1, 0, 3 if way == 0 else 1, 0))
-        def _(way=way):
-            p(1, way).wait_recv()
-            spread(1, 3 if way == 0 else 1)
-
-        for a in range(4):
-            @event((0, 0, a, 3 if way == 0 else 1))
-            def _(a=a, way=way):
-                q(0, a, way).wait_recv()
-                q2(a, way).start()
-                across(0, a, 3 if way == 0 else 1).start()
-
-            @event((1, 0, a, 3 if way == 0 else 1))
-            def _(a=a, way=way):
-                q(1, a, way).wait_recv()
-                across(1, a, 3 if way == 0 else 1).start()
-
-    @event((1, 0, 0, 0))
-    def _():
-        down(0, 0).wait_recv()
-        p(1, 0).start()
-        p(1, 1).start()
-        spread(1, 0)
-
-    @event((0, 0, 2, 0))
-    def _():
-        p2(0).wait_recv()
-        p2(1).wait_recv()
-        down(2, 0).start()
-        spread(0, 2)
-
-    @event((1, 0, 2, 0))
-    def _():
-        down(2, 0).wait_recv()
-        spread(1, 2)
-
-    for a in range(4):
-        @event((0, 0, a, 2))
-        def _(a=a):
-            q2(a, 0).wait_recv()
-            q2(a, 1).wait_recv()
-            down(a, 2).start()
-            across(0, a, 2).start()
-
-        @event((1, 0, a, 2))
-        def _(a=a):
-            down(a, 2).wait_recv()
-            across(1, a, 2).start()
-
-        for r in range(2):
-            for b in range(4):
-                @event((r, 1, a, b))
-                def _(r=r, a=a, b=b):
-                    across(r, a, b).wait_recv()
-
-    acts = {PLACE[tile]: act for (tile,), act in arrivals.items()}
-
     @pl.loop(0, WINDOW // GROUP)
     def _(i):
         def dispatch(first, last):
             if last - first == 1:
                 for n in range(first * GROUP, last * GROUP):
-                    if n:
+                    if n > early:
                         acts[n]()
                 return
             middle = (first + last) // 2

time: 69.2 us -> 69.2 us (level)
  no operation moved by 1% of the time
where the time goes in v5:
time: 69.2 us; the launch traced here: 69.1 us
  Pallas kernels  65.9 us (95%)
  other arithmetic  1.86 us (3%)
  between operations  1.29 us (2%)
    pallas_call x1, Pallas kernels, shards(): pl.pallas_call(kernel, out_shape=(jax.ShapeDtypeStruct((8, 128), F32), ja...  65.9 us

profile of v5, /device:TPU:1, one launch (start us, length us, event | category | flops | bytes accessed | tf_op | source)
XLA Modules:
  0.0 69.1 jit_solution(12669634467447583489)
XLA Ops:
  1.3 65.9 %shard_map.68 = (f32[8,128]{1,0:T(8,128)}, f32[2,128]{1,0:T(2,128)}) custom-call(bf16[1024,256]{1,0:T(8,128)(2,1)} %source_in.1, bf16[256,256]{1,0:T(8,128)(2,1)} %target_in.1, s32[1,128]{1,0:T(1,128)} %pair_source.1, s32[1,128]{1,0:T(1,128)} %pair_target.1, s32[1]{0:T(128)S(6)} %copy.7.pair_count), custom_call_target="tpu_custom_call" | custom-call | tf_op jit(solution)/shard_map/pallas_call | solution.py:393
  67.2 0.0 copy-start
  67.2 1.3 %log_bitcast_fusion = f32[1024]{0:T(1024)} fusion(f32[8,128]{1,0:T(8,128)} %get-tuple-element.4), kind=kLoop, calls=%fused_computation | loop fusion | flops 1024 | bytes 8192 | tf_op jit(solution)/shard_map/log | solution.py:431
  68.5 0.0 copy-done
  68.5 0.6 log_bitcast_fusion.1
Async XLA Ops:
  67.2 1.3 %copy-start = (f32[2,128]{1,0:T(2,128)S(1)}, f32[2,128]{1,0:T(2,128)}, u32[]{:S(2)}) copy-start(f32[2,128]{1,0:T(2,128)} %get-tuple-element.5) | copy-start | bytes 3076
